TPU v7x, 512 devices: a whole 4x4x16 slice. The times are simulated.
512 devices in a mesh: elem: 512 (over z, y, x, core).
Axes of the slice: x: 4, y: 4, z: 16, core: 2. Of those that a mesh axis runs over, the one named last changes fastest.
Arguments:
- right_side: float32 [2048, 320], P('elem'), may hold values from -6 to 6
- diag_blocks: float32 [2048, 320, 320], P('elem')
- face_blocks: float32 [2048, 6, 80, 80], P('elem'), may hold values from -0.15625 to 0.15625
- neighbours: int32 [2048, 6], P('elem'), may hold values from -1 to 2047, as said below
Outputs:
- basis_q: float32 [2048, 5, 320], P('elem')
- r_factor: float32 [5, 5], replicated
- update: float32 [2048, 320], P('elem')
Inputs may be any that keep to these rules, and one draw needn't show every extreme that they name: Neighbours are mutual: if neighbours[e, f] = g >= 0 then neighbours[g, f xor 1] = e. Element e lies on device e // 4; across faces 0 and 1 the neighbour lies on the device before and after it, across faces 2 to 5 on the same device. Facing nodes of the two elements match in order.
All inputs are finite; a program needn't handle non-finite values.
Results may differ from a plain program's by a relative error of at most 0.0034.
Values sent between devices are 32-bit elements; how exact they have to be, the bound alone decides.
A program may use at most 64 MiB of HBM per device.

v0:
```python
import jax
import jax.numpy as jnp
from jax import lax
from jax.sharding import PartitionSpec as P

FIELDS = 5
ORDER = 3
POWERS = 4
BASIS = 5


OPPOSITE = (1, 0, 3, 2, 5, 4)


def with_halo(block, sides, width):
    for axis, dim in sides:
        count = lax.axis_size(axis)
        forward = [(i, i + 1) for i in range(count - 1)]
        backward = [(target, source) for source, target in forward]
        low = lax.ppermute(
            lax.slice_in_dim(block, block.shape[dim] - width, None, axis=dim), axis, forward
        )
        high = lax.ppermute(lax.slice_in_dim(block, 0, width, axis=dim), axis, backward)
        block = jnp.concatenate([low, block, high], axis=dim)
    return block


def partner_2(value, axis, distance):
    mask = 2**distance
    pairs = [(source, source ^ mask) for source in range(lax.axis_size(axis))]
    return lax.ppermute(value, axis, pairs)


def face_traces(cube):
    count = cube.shape[0]
    sides = [
        cube[:, :, 0],
        cube[:, :, ORDER],
        cube[:, :, :, 0],
        cube[:, :, :, ORDER],
        cube[:, :, :, :, 0],
        cube[:, :, :, :, ORDER],
    ]
    return [side.reshape(count, -1) for side in sides]


def add_faces(cube, contrib):
    count = cube.shape[0]
    shape = (count, FIELDS, ORDER + 1, ORDER + 1)
    cube = cube.at[:, :, 0].add(contrib[:, 0].reshape(shape))
    cube = cube.at[:, :, ORDER].add(contrib[:, 1].reshape(shape))
    cube = cube.at[:, :, :, 0].add(contrib[:, 2].reshape(shape))
    cube = cube.at[:, :, :, ORDER].add(contrib[:, 3].reshape(shape))
    cube = cube.at[:, :, :, :, 0].add(contrib[:, 4].reshape(shape))
    cube = cube.at[:, :, :, :, ORDER].add(contrib[:, 5].reshape(shape))
    return cube


def pick_rows(table, wanted, offset):
    count = table.shape[0]
    local = jnp.clip(wanted - offset, 0, count - 1)
    return jnp.where((wanted >= 0)[:, None], table[local], jnp.float32(0.0))


def operate(vector, diag_blocks, face_blocks, neighbours, base):
    count = vector.shape[0]
    cube = vector.reshape(count, FIELDS, ORDER + 1, ORDER + 1, ORDER + 1)
    traces = face_traces(cube)
    outgoing = jnp.stack([traces[0], traces[1]], 0)
    padded = with_halo(outgoing, (("elem", 0),), 1)
    gathered = [
        pick_rows(padded[0], neighbours[:, 0], base - count),
        pick_rows(padded[3], neighbours[:, 1], base + count),
    ]
    for face in range(2, 6):
        gathered.append(pick_rows(traces[OPPOSITE[face]], neighbours[:, face], base))
    incoming = jnp.stack(gathered, 1)
    contrib = jnp.einsum("efab,efb->efa", face_blocks, incoming, precision=lax.Precision.HIGHEST)
    own = jnp.einsum("eab,eb->ea", diag_blocks, vector, precision=lax.Precision.HIGHEST)
    return add_faces(own.reshape(cube.shape), contrib).reshape(count, -1)


def lower_cholesky(matrix):
    size = matrix.shape[0]
    entries = [[jnp.float32(0.0) for across in range(size)] for below in range(size)]
    for column in range(size):
        total = matrix[column, column]
        for inner in range(column):
            total = total - entries[column][inner] * entries[column][inner]
        pivot = jnp.sqrt(total)
        entries[column][column] = pivot
        for below in range(column + 1, size):
            value = matrix[below, column]
            for inner in range(column):
                value = value - entries[below][inner] * entries[column][inner]
            entries[below][column] = value / pivot
    return jnp.stack([jnp.stack(line) for line in entries])


def upper_inverse(factor):
    size = factor.shape[0]
    entries = [[jnp.float32(0.0) for across in range(size)] for below in range(size)]
    for column in range(size):
        for outer in range(size - 1, -1, -1):
            value = jnp.float32(1.0) if outer == column else jnp.float32(0.0)
            for inner in range(outer + 1, size):
                value = value - factor[outer, inner] * entries[inner][column]
            entries[outer][column] = value / factor[outer, outer]
    return jnp.stack([jnp.stack(line) for line in entries])


def forward_solve(lower, target):
    size = lower.shape[0]
    values = []
    for outer in range(size):
        value = target[outer]
        for inner in range(outer):
            value = value - lower[outer, inner] * values[inner]
        values.append(value / lower[outer, outer])
    return jnp.stack(values)


def backward_solve(upper, target):
    size = upper.shape[0]
    values = [jnp.float32(0.0)] * size
    for outer in range(size - 1, -1, -1):
        value = target[outer]
        for inner in range(outer + 1, size):
            value = value - upper[outer, inner] * values[inner]
        values[outer] = value / upper[outer, outer]
    return jnp.stack(values)


def cholesky_factor(colmat):
    gram = jnp.dot(colmat, colmat.T, precision=lax.Precision.HIGHEST)
    first = lower_cholesky(gram).T
    cleaned = jnp.dot(upper_inverse(first).T, colmat, precision=lax.Precision.HIGHEST)
    gram_two = jnp.dot(cleaned, cleaned.T, precision=lax.Precision.HIGHEST)
    second = lower_cholesky(gram_two).T
    return jnp.dot(second, first, precision=lax.Precision.HIGHEST)


def small_solve(r_factor):
    square = r_factor[:POWERS, :POWERS]
    tail = r_factor[:, 1:]
    square_inverse = upper_inverse(square)
    hess = jnp.dot(tail, square_inverse, precision=lax.Precision.HIGHEST)
    normal = jnp.dot(hess.T, hess, precision=lax.Precision.HIGHEST)
    target = r_factor[0, 0] * hess[0, :]
    lower = lower_cholesky(normal)
    middle = forward_solve(lower, target)
    solved = backward_solve(lower.T, middle)
    return jnp.dot(square_inverse, solved, precision=lax.Precision.HIGHEST)


def body(right_side, diag_blocks, face_blocks, neighbours):
    count, width = right_side.shape
    base = lax.axis_index("elem") * count
    vector = right_side
    basis = [vector]
    for power in range(POWERS):
        vector = operate(vector, diag_blocks, face_blocks, neighbours, base)
        basis.append(vector)
    stacked = jnp.stack(basis, 1)
    colmat = stacked.transpose(1, 0, 2).reshape(BASIS, -1)
    r_factor = cholesky_factor(colmat)
    levels = lax.axis_size("elem").bit_length() - 1
    for bit in range(levels):
        partner = partner_2(r_factor, "elem", bit)
        upper_side = lax.axis_index("elem") // 2**bit % 2 == 1
        lower_part = jnp.where(upper_side, partner, r_factor)
        upper_part = jnp.where(upper_side, r_factor, partner)
        r_factor = cholesky_factor(jnp.concatenate([lower_part, upper_part], 0).T)
    q_rows = jnp.dot(upper_inverse(r_factor).T, colmat, precision=lax.Precision.HIGHEST)
    basis_q = q_rows.reshape(BASIS, count, width).transpose(1, 0, 2)
    coeffs = small_solve(r_factor)
    update = jnp.einsum("k,ekm->em", coeffs, stacked[:, :POWERS], precision=lax.Precision.HIGHEST)
    return (basis_q, r_factor, update)


def solution(mesh):
    in_specs = (
        P("elem", None),
        P("elem", None, None),
        P("elem", None, None, None),
        P("elem", None),
    )
    out_specs = (P("elem", None, None), P(), P("elem", None))
    return jax.shard_map(body, mesh=mesh, in_specs=in_specs, out_specs=out_specs, check_vma=False)
```

profile of v0, /device:TPU:62, one launch (start us, length us, event | category | flops | bytes accessed | tf_op | source)
XLA Modules:
  0.0 819.1 jit_solution(15858397198210962717)
XLA Ops:
  1.9 1.9 collective-permute-start
  3.9 3.6 collective-permute-start.1
  9.1 2.5 fusion.25
  16.7 1.6 fusion.23
  20.9 6.0 scatter-add.89
  27.3 1.8 fusion.172
  29.2 1.9 collective-permute-start.2
  31.9 3.8 collective-permute-start.3
  45.3 6.0 scatter-add.99
  51.7 1.8 fusion.173
  53.7 8.5 %collective-permute-start.4 = (f32[1,4,80]{2,1,0:T(4,128)S(1)}, f32[1,4,80]{2,1,0:T(4,128)S(1)}, u32[]{:S(2)}, u32[]{:S(2)}) collective-permute-start(f32[1,4,80]{2,1,0:T(4,128)S(1)} %stack_reshape_squeeze.28), channel_id=1, source_target_pairs={{0,1},{1,2},{2,3},{3,4},{4,5},{5,6},{6,7},{7,8},{8,9},{9,10},{10,1... | collective-permute-start | bytes 3848 | tf_op jit(solution)/shard_map/ppermute | solution.py:20
  62.9 1.9 collective-permute-start.5
  73.2 6.2 scatter-add.109
  79.8 1.8 fusion.174
  81.7 8.0 collective-permute-start.6
  90.5 1.9 collective-permute-start.7
  100.6 6.0 scatter-add.119
  162.5 7.9 collective-permute-start.8
  226.5 1.9 collective-permute-start.9
  228.4 3.6 collective-permute-done.9
  287.3 2.2 collective-permute-start.10
  289.5 4.8 collective-permute-done.10
  349.6 1.9 collective-permute-start.11
  351.5 3.6 collective-permute-done.11
  410.4 1.9 collective-permute-start.12
  412.4 5.1 collective-permute-done.12
  472.7 2.0 collective-permute-start.13
  474.8 3.5 collective-permute-done.13
  533.5 11.2 %collective-permute-start.14 = (f32[5,5]{0,1:T(8,128)S(1)}, f32[5,5]{0,1:T(8,128)S(1)}, u32[]{:S(2)}, u32[]{:S(2)}) collective-permute-start(f32[5,5]{0,1:T(8,128)S(1)} %fusion.189), channel_id=1, source_target_pairs={{0,64},{1,65},{2,66},{3,67},{4,68},{5,69},{6,70},{7,71},{8,72},{9,... | collective-permute-start | bytes 308 | tf_op jit(solution)/shard_map/ppermute | solution.py:31
  601.6 9.1 %collective-permute-start.15 = (f32[5,5]{0,1:T(8,128)S(1)}, f32[5,5]{0,1:T(8,128)S(1)}, u32[]{:S(2)}, u32[]{:S(2)}) collective-permute-start(f32[5,5]{0,1:T(8,128)S(1)} %fusion.191), channel_id=1, source_target_pairs={{0,128},{1,129},{2,130},{3,131},{4,132},{5,133},{6,134},{7,135},{8... | collective-permute-start | bytes 308 | tf_op jit(solution)/shard_map/ppermute | solution.py:31
  667.6 9.7 %collective-permute-start.16 = (f32[5,5]{0,1:T(8,128)S(1)}, f32[5,5]{0,1:T(8,128)S(1)}, u32[]{:S(2)}, u32[]{:S(2)}) collective-permute-start(f32[5,5]{0,1:T(8,128)S(1)} %fusion.193), channel_id=1, source_target_pairs={{0,256},{1,257},{2,258},{3,259},{4,260},{5,261},{6,262},{7,263},{8... | collective-permute-start | bytes 308 | tf_op jit(solution)/shard_map/ppermute | solution.py:31
  677.4 4.5 collective-permute-done.16
  (475 shorter events, 91.7 us)
Async XLA Ops:
  0.6 8.4 %copy-start = (f32[4,320,320]{2,1,0:T(8,128)S(1)}, f32[4,320,320]{2,1,0:T(8,128)}, u32[]{:S(2)}) copy-start(f32[4,320,320]{2,1,0:T(8,128)} %param.53) | copy-start | bytes 4915204
  0.6 11.0 %copy-start.2 = (s32[4,6]{1,0:T(4,128)S(1)}, s32[4,6]{1,0:T(4,128)}, u32[]{:S(2)}) copy-start(s32[4,6]{1,0:T(4,128)} %param.55) | copy-start | bytes 292
  0.7 16.1 %copy-start.1 = (f32[4,6,80,80]{3,2,1,0:T(8,128)S(1)}, f32[4,6,80,80]{3,2,1,0:T(8,128)}, u32[]{:S(2)}) copy-start(f32[4,6,80,80]{3,2,1,0:T(8,128)} %param.54) | copy-start | bytes 1843204
  1.9 13.3 %collective-permute-start = (f32[1,4,80]{2,1,0:T(4,128)S(1)}, f32[1,4,80]{2,1,0:T(4,128)S(1)}, u32[]{:S(2)}, u32[]{:S(2)}) collective-permute-start(f32[1,4,80]{2,1,0:T(4,128)S(1)} %stack_reshape_squeeze.24), channel_id=1, source_target_pairs={{0,1},{1,2},{2,3},{3,4},{4,5},{5,6},{6,7},{7,8},{8,9},{9,10},{10,1... | collective-permute-start | bytes 3848 | tf_op jit(solution)/shard_map/ppermute | solution.py:20
  3.9 11.9 %collective-permute-start.1 = (f32[1,4,80]{2,1,0:T(4,128)S(1)}, f32[1,4,80]{2,1,0:T(4,128)S(1)}, u32[]{:S(2)}, u32[]{:S(2)}) collective-permute-start(f32[1,4,80]{2,1,0:T(4,128)S(1)} %stack_reshape_squeeze.25), channel_id=1, source_target_pairs={{1,0},{2,1},{3,2},{4,3},{5,4},{6,5},{7,6},{8,7},{9,8},{10,9},{11,1... | collective-permute-start | bytes 3848 | tf_op jit(solution)/shard_map/ppermute | solution.py:23
  29.2 9.1 %collective-permute-start.2 = (f32[1,4,80]{2,1,0:T(4,128)S(1)}, f32[1,4,80]{2,1,0:T(4,128)S(1)}, u32[]{:S(2)}, u32[]{:S(2)}) collective-permute-start(f32[1,4,80]{2,1,0:T(4,128)S(1)} %stack_reshape_squeeze.26), channel_id=1, source_target_pairs={{0,1},{1,2},{2,3},{3,4},{4,5},{5,6},{6,7},{7,8},{8,9},{9,10},{10,1... | collective-permute-start | bytes 3848 | tf_op jit(solution)/shard_map/ppermute | solution.py:20
  31.9 8.4 %collective-permute-start.3 = (f32[1,4,80]{2,1,0:T(4,128)S(1)}, f32[1,4,80]{2,1,0:T(4,128)S(1)}, u32[]{:S(2)}, u32[]{:S(2)}) collective-permute-start(f32[1,4,80]{2,1,0:T(4,128)S(1)} %stack_reshape_squeeze.27), channel_id=1, source_target_pairs={{1,0},{2,1},{3,2},{4,3},{5,4},{6,5},{7,6},{8,7},{9,8},{10,9},{11,1... | collective-permute-start | bytes 3848 | tf_op jit(solution)/shard_map/ppermute | solution.py:23
  53.7 13.8 %collective-permute-start.4 = (f32[1,4,80]{2,1,0:T(4,128)S(1)}, f32[1,4,80]{2,1,0:T(4,128)S(1)}, u32[]{:S(2)}, u32[]{:S(2)}) collective-permute-start(f32[1,4,80]{2,1,0:T(4,128)S(1)} %stack_reshape_squeeze.28), channel_id=1, source_target_pairs={{0,1},{1,2},{2,3},{3,4},{4,5},{5,6},{6,7},{7,8},{8,9},{9,10},{10,1... | collective-permute-start | bytes 3848 | tf_op jit(solution)/shard_map/ppermute | solution.py:20
  62.9 5.2 collective-permute-start.5
  81.7 13.3 %collective-permute-start.6 = (f32[1,4,80]{2,1,0:T(4,128)S(1)}, f32[1,4,80]{2,1,0:T(4,128)S(1)}, u32[]{:S(2)}, u32[]{:S(2)}) collective-permute-start(f32[1,4,80]{2,1,0:T(4,128)S(1)} %stack_reshape_squeeze.30), channel_id=1, source_target_pairs={{0,1},{1,2},{2,3},{3,4},{4,5},{5,6},{6,7},{7,8},{8,9},{9,10},{10,1... | collective-permute-start | bytes 3848 | tf_op jit(solution)/shard_map/ppermute | solution.py:20
  90.5 5.2 collective-permute-start.7
  162.5 8.7 %collective-permute-start.8 = (f32[5,5]{0,1:T(8,128)S(1)}, f32[5,5]{0,1:T(8,128)S(1)}, u32[]{:S(2)}, u32[]{:S(2)}) collective-permute-start(f32[5,5]{0,1:T(8,128)S(1)} %fusion.177), channel_id=1, source_target_pairs={{0,1},{1,0},{2,3},{3,2},{4,5},{5,4},{6,7},{7,6},{8,9},{9,8},{10,11... | collective-permute-start | bytes 308 | tf_op jit(solution)/shard_map/ppermute | solution.py:31
  226.5 5.5 collective-permute-start.9
  287.3 7.0 collective-permute-start.10
  349.6 5.5 collective-permute-start.11
  410.4 7.0 collective-permute-start.12
  472.7 5.5 collective-permute-start.13
  533.5 12.8 %collective-permute-start.14 = (f32[5,5]{0,1:T(8,128)S(1)}, f32[5,5]{0,1:T(8,128)S(1)}, u32[]{:S(2)}, u32[]{:S(2)}) collective-permute-start(f32[5,5]{0,1:T(8,128)S(1)} %fusion.189), channel_id=1, source_target_pairs={{0,64},{1,65},{2,66},{3,67},{4,68},{5,69},{6,70},{7,71},{8,72},{9,... | collective-permute-start | bytes 308 | tf_op jit(solution)/shard_map/ppermute | solution.py:31
  601.6 10.7 %collective-permute-start.15 = (f32[5,5]{0,1:T(8,128)S(1)}, f32[5,5]{0,1:T(8,128)S(1)}, u32[]{:S(2)}, u32[]{:S(2)}) collective-permute-start(f32[5,5]{0,1:T(8,128)S(1)} %fusion.191), channel_id=1, source_target_pairs={{0,128},{1,129},{2,130},{3,131},{4,132},{5,133},{6,134},{7,135},{8... | collective-permute-start | bytes 308 | tf_op jit(solution)/shard_map/ppermute | solution.py:31
  667.6 14.2 %collective-permute-start.16 = (f32[5,5]{0,1:T(8,128)S(1)}, f32[5,5]{0,1:T(8,128)S(1)}, u32[]{:S(2)}, u32[]{:S(2)}) collective-permute-start(f32[5,5]{0,1:T(8,128)S(1)} %fusion.193), channel_id=1, source_target_pairs={{0,256},{1,257},{2,258},{3,259},{4,260},{5,261},{6,262},{7,263},{8... | collective-permute-start | bytes 308 | tf_op jit(solution)/shard_map/ppermute | solution.py:31
where the time goes:
time: 835 us; the launch traced here: 819 us
  between operations  589 us (71%)
  local copies, waits for them, and re-layouts  91 us (11%)
  starting transfers between devices  79.5 us (10%)
  waiting for transfers between devices  30.1 us (4%)
  matrix products  22.1 us (3%)
    ppermute x9, starting transfers between devices, partner_2(): return lax.ppermute(value, axis, pairs)  47.8 us
    ppermute x9, waiting for transfers between devices, partner_2(): return lax.ppermute(value, axis, pairs)  28.9 us
    scatter-add x4, local copies, waits for them, and re-layouts, add_faces(): cube = cube.at[:, :, :, :, ORDER].add(contrib[:, 5].reshape(shape))  24.1 us
    ppermute x4, starting transfers between devices, with_halo(): lax.ppermute(lax.slice_in_dim(block, block.shape[dim] - width, None, axis...  20.4 us
  transfers between devices with their start and end apart: 17, of which 10 were waited for; matrix products, arithmetic and copies ran while one was open for 2% of the time, Pallas kernels for 0%

commit v1 on v0

v1 whole, which is shorter than its diff:
```python
import jax
import jax.numpy as jnp
from jax import lax
from jax.experimental import pallas as pl
from jax.experimental.pallas import tpu as pltpu
from jax.sharding import PartitionSpec as P

POWERS = 4
BASIS = 5
ELEM_DEV = 4
WIDTH = 320
FACE_WIDTH = 80
N_DEV = 512
PLANE = 32
N_Z = 16
F32 = jnp.float32
MESH = pl.DeviceIdType.MESH


def iota(shape, dim):
    return lax.broadcasted_iota(jnp.int32, shape, dim)


def two_sum(a, b):
    s = a + b
    t = s - a
    return s, (a - (s - t)) + (b - t)


def fast_two_sum(a, b):
    s = a + b
    return s, b - (s - a)


def split(a):
    c = a * 4097.0
    high = c - (c - a)
    return high, a - high


def two_prod(a, b):
    p = a * b
    ah, al = split(a)
    bh, bl = split(b)
    return p, ((ah * bh - p) + ah * bl + al * bh) + al * bl


def trace_tiles(tiles):
    lane = iota((8, 128), 1)
    within, field_odd = lane % 16, (lane // 16) % 2
    u, w = within // 4, within % 4
    offsets = [
        4 * u + w,
        48 + 4 * u + w,
        16 * u + w,
        16 * u + 12 + w,
        16 * u + 4 * w,
        16 * u + 4 * w + 3,
    ]
    out = []
    for offset in offsets:
        index = field_odd * 64 + offset
        got = [jnp.take_along_axis(tile, index, axis=1) for tile in tiles]
        out.append(jnp.where(lane < 32, got[0], jnp.where(lane < 64, got[1], got[2])))
    return out


def face_lane(face, rows, first):
    a = iota((rows, 128), 0) + first
    field_odd, within = (a // 16) % 2, a % 16
    u, w = within // 4, within % 4
    offset = [
        4 * u + w,
        48 + 4 * u + w,
        16 * u + w,
        16 * u + 12 + w,
        16 * u + 4 * w,
        16 * u + 4 * w + 3,
    ][face]
    return field_odd * 64 + offset


def fold(placed):
    return jnp.sum(placed.reshape(-1, 8, 128), axis=0)


def place_element(column):
    out = []
    for tile in range(3):
        rows = min(128, WIDTH - 128 * tile)
        part = jnp.broadcast_to(column[128 * tile : 128 * tile + rows], (rows, 128))
        out.append(fold(jnp.where(iota((rows, 128), 0) == iota((rows, 128), 1), part, 0.0)))
    return out


def place_face(face, column):
    out = []
    for tile in range(3):
        rows = min(32, FACE_WIDTH - 32 * tile)
        part = jnp.broadcast_to(column[32 * tile : 32 * tile + rows], (rows, 128))
        out.append(fold(jnp.where(face_lane(face, rows, 32 * tile) == iota((rows, 128), 1), part, 0.0)))
    return out


def place_trace(column):
    shape = (FACE_WIDTH, 128)
    part = jnp.broadcast_to(column, shape)
    return jnp.sum(jnp.where(iota(shape, 0) == iota(shape, 1), part, 0.0), axis=0, keepdims=True)


def add_all(left, right):
    return [a + b for a, b in zip(left, right)]


def matvec(matrix, row):
    return jnp.sum(matrix * row, axis=1, keepdims=True)


def gram_column(basis, k):
    chains = []
    for tile in range(3):
        total, low = None, None
        for e in range(ELEM_DEV):
            x = basis[e, :, 128 * tile : 128 * tile + 128]
            b = jnp.broadcast_to(basis[e, k : k + 1, 128 * tile : 128 * tile + 128], (8, 128))
            p, err = two_prod(x, b)
            if total is None:
                total, low = p, err
            else:
                total, more = two_sum(total, p)
                low = low + (err + more)
        chains.append((total, low))
    total, low = chains[0]
    for other, other_low in chains[1:]:
        total, more = two_sum(total, other)
        low = low + (other_low + more)
    for shift in (64, 32, 16, 8, 4, 2, 1):
        other, other_low = pltpu.roll(total, shift, 1), pltpu.roll(low, shift, 1)
        total, more = two_sum(total, other)
        low = (low + other_low) + more
    return total, low


def pack(message, k, pair):
    lane = iota((8, 128), 1)
    message = jnp.where(lane == k, pair[0], message)
    return jnp.where(lane == 8 + k, pair[1], message)


def sum_messages(tiles):
    chains = []
    for start in range(4):
        mine = tiles[start::4]
        total, low = mine[0], jnp.zeros((8, 128), F32)
        for tile in mine[1:]:
            total, more = two_sum(total, tile)
            low = low + more
        chains.append((total, low))
    while len(chains) > 1:
        merged = []
        for a, b in zip(chains[::2], chains[1::2]):
            total, more = two_sum(a[0], b[0])
            merged.append((total, (a[1] + b[1]) + more))
        chains = merged
    total, low = chains[0]
    return fast_two_sum(total, low + pltpu.roll(total, 120, 1))


def repack(high, low):
    return jnp.where(iota((8, 128), 1) < 8, high, pltpu.roll(low, 8, 1))


def solve(high, low):
    def spread(tile, i, k):
        return jnp.broadcast_to(tile[i : i + 1, k : k + 1], (8, 128))

    g = {(i, k): (spread(high, i, k), spread(low, i, k)) for i in range(BASIS) for k in range(i, BASIS)}
    factors, inverse, r = {}, [], {}
    for j in range(BASIS):
        d, d_low = g[j, j]
        root = lax.rsqrt(d)
        root = root * (1.5 - 0.5 * d * root * root)
        inverse.append(root)
        for k in range(j, BASIS):
            r[j, k] = g[j, k][0] * root
        if j == BASIS - 1:
            break
        recip = 1.0 / d
        ls = {}
        for i in range(j + 1, BASIS):
            t, t_low = g[j, i]
            first = t * recip
            p, err = two_prod(first, d)
            rest = (((t - p) - err) + t_low) - first * d_low
            ls[i] = fast_two_sum(first, rest * recip)
            factors[i, j] = ls[i][0]
        for i in range(j + 1, BASIS):
            for k in range(i, BASIS):
                t, t_low = g[j, k]
                p, err = two_prod(ls[i][0], t)
                err = err + (ls[i][0] * t_low + ls[i][1] * t)
                total, more = two_sum(g[i, k][0], -p)
                g[i, k] = fast_two_sum(total, more + (g[i, k][1] - err))
    h = {}
    for j in range(POWERS):
        for i in range(j + 2):
            value = r[i, j + 1]
            for m in range(max(i - 1, 0), j):
                value = value - h[i, m] * r[m, j]
            h[i, j] = value * inverse[j]
    normal = {}
    for a in range(POWERS):
        for b in range(a, POWERS):
            value = h[0, a] * h[0, b]
            for i in range(1, a + 2):
                value = value + h[i, a] * h[i, b]
            normal[a, b] = value
    target = [r[0, 0] * h[0, a] for a in range(POWERS)]
    lower, recips = {}, []
    for j in range(POWERS):
        recips.append(1.0 / normal[j, j])
        for i in range(j + 1, POWERS):
            lower[i, j] = normal[j, i] * recips[j]
        for i in range(j + 1, POWERS):
            target[i] = target[i] - lower[i, j] * target[j]
            for k in range(i, POWERS):
                normal[i, k] = normal[i, k] - lower[i, j] * normal[j, k]
    y = [target[j] * recips[j] for j in range(POWERS)]
    for j in range(POWERS - 1, -1, -1):
        for i in range(j + 1, POWERS):
            y[j] = y[j] - lower[i, j] * y[i]
    return factors, r, inverse, y


def kernel(
    nb_ref, rhs_ref, diag_hbm, face_hbm,
    q_ref, r_ref, up_ref,
    diag, face, basis, rows, traces, out_x, in_a, in_b, in_c, in_d, far, message, got_plane, got_z,
    load_sem, far_send, far_recv, x_send, x_recv, p_send, p_recv, z_send, z_recv,
):
    in_x = ((in_a, in_b), (in_c, in_d))
    me = lax.axis_index("elem")
    place, z, core = me % PLANE, me // PLANE, me % 2
    plane0 = me - place

    loads = [
        pltpu.make_async_copy(diag_hbm, diag, load_sem.at[0]),
        pltpu.make_async_copy(face_hbm, face, load_sem.at[1]),
    ]
    for load in loads:
        load.start()

    barrier = pltpu.get_barrier_semaphore()

    def greet(device):
        pl.semaphore_signal(barrier, inc=1, device_id=(device,), device_id_type=MESH)

    for d in range(1, N_Z):
        greet(((z + d) % N_Z) * PLANE + place - core + 1)

    @pl.when(core == 1)
    def _():
        for d in range(1, PLANE):
            greet(plane0 + (place + d) % PLANE)

        @pl.when(jnp.logical_and(place == PLANE - 1, me < N_DEV - 1))
        def _():
            greet(me + 1)

    @pl.when(core == 0)
    def _():
        greet(me + 1)

        @pl.when(me > 0)
        def _():
            greet(me - 1)

    basis[...] = jnp.zeros(basis.shape, F32)
    rows[...] = jnp.zeros(rows.shape, F32)
    rows[0:ELEM_DEV, 0:WIDTH] = rhs_ref[...]

    def store_row(k, e, tiles):
        for t in range(3):
            lanes = min(128, WIDTH - 128 * t)
            row = jnp.sum(tiles[t], axis=0, keepdims=True)[:, :lanes]
            basis[e, k : k + 1, 128 * t : 128 * t + lanes] = row
            rows[e : e + 1, 128 * t : 128 * t + lanes] = row

    def make_traces():
        got = trace_tiles([rows[:, 128 * t : 128 * t + 128] for t in range(3)])
        for f in range(6):
            traces[f] = got[f]

    for e in range(ELEM_DEV):
        basis[e, 0:1, 0:WIDTH] = rhs_ref[e : e + 1, :]
    make_traces()

    def x_traces(tiles):
        got = trace_tiles(tiles)
        return got[0], got[1]

    def send_x(step, kind):
        for side in range(2):
            @pl.when(me > 0 if side == 0 else me < N_DEV - 1)
            def _():
                x_copy(step, kind, side).start()

    def x_copy(step, kind, side):
        return pltpu.make_async_remote_copy(
            src_ref=out_x.at[step, kind, side],
            dst_ref=in_x[step][kind].at[1 - side],
            send_sem=x_send.at[step, kind, side],
            recv_sem=x_recv.at[step, kind, 1 - side],
            device_id=(me - 1 if side == 0 else me + 1,),
            device_id_type=MESH,
        )

    def wait_x(step, kind):
        for side in range(2):
            @pl.when(me < N_DEV - 1 if side == 0 else me > 0)
            def _():
                x_copy(step, kind, side).wait_recv()

    def far_copy(side):
        return pltpu.make_async_remote_copy(
            src_ref=face.at[:, side],
            dst_ref=far.at[1 - side],
            send_sem=far_send.at[side],
            recv_sem=far_recv.at[1 - side],
            device_id=(me - 1 if side == 0 else me + 1,),
            device_id_type=MESH,
        )

    heard = jnp.where(
        core == 1,
        (N_Z - 1) * 2 + 15 + 2 - jnp.where(me == N_DEV - 1, 1, 0),
        16 + jnp.where(jnp.logical_and(place == 0, me > 0), 1, 0),
    )
    pl.semaphore_wait(barrier, heard)

    out_x[0, 0, 0] = traces[0]
    out_x[0, 0, 1] = traces[1]
    send_x(0, 0)
    loads[1].wait()
    for side in range(2):
        @pl.when(me > 0 if side == 0 else me < N_DEV - 1)
        def _():
            far_copy(side).start()
    loads[0].wait()

    base = me * ELEM_DEV

    def link(e, f):
        wanted = nb_ref[e, f]
        first = base + (-ELEM_DEV if f == 0 else ELEM_DEV if f == 1 else 0)
        return wanted >= 0, jnp.clip(wanted - first, 0, ELEM_DEV - 1)

    links = [[link(e, f) for f in range(6)] for e in range(ELEM_DEV)]

    def own_part(out):
        for e in range(ELEM_DEV):
            total = place_element(matvec(diag[e], rows[e : e + 1, 0:WIDTH]))
            for f in range(2, 6):
                valid, index = links[e][f]
                row = jnp.where(valid, traces[f ^ 1, pl.ds(index, 1), :], 0.0)
                total = add_all(total, place_face(f, matvec(face[e, f], row[:, 0:FACE_WIDTH])))
            out.append(total)

    def x_part(e, across):
        total = None
        for f in range(2):
            part = place_face(f, matvec(face[e, f], across[f][:, 0:FACE_WIDTH]))
            total = part if total is None else add_all(total, part)
        return total

    def received(step, kind, e, f):
        valid, index = links[e][f]
        return valid, in_x[step][kind][f, pl.ds(index, 1), :]

    grams = {}
    for step in range(2):
        k = 2 * step
        own = []
        own_part(own)
        sums = [
            jnp.concatenate([jnp.sum(own[e][t], axis=0, keepdims=True) for e in range(ELEM_DEV)] * 2, axis=0)
            for t in range(3)
        ]
        low, high = x_traces(sums)
        out_x[step, 1, 0] = low
        out_x[step, 1, 1] = high
        send_x(step, 1)
        if step == 0:
            for side in range(2):
                @pl.when(me < N_DEV - 1 if side == 0 else me > 0)
                def _():
                    far_copy(side).wait_recv()
        back = []
        for e in range(ELEM_DEV):
            pair = []
            for f in range(2):
                valid, index = links[e][f]
                trace = traces[f, e : e + 1, 0:FACE_WIDTH]
                pair.append(place_trace(matvec(far[f, index], trace)))
            back.append(pair)
        if step == 1:
            for kk in range(3):
                grams[kk] = gram_column(basis, kk)
        wait_x(step, 0)
        for e in range(ELEM_DEV):
            across = []
            for f in range(2):
                valid, row = received(step, 0, e, f)
                across.append(jnp.where(valid, row, 0.0))
            store_row(k + 1, e, add_all(own[e], x_part(e, across)))
        make_traces()
        own = []
        own_part(own)
        wait_x(step, 1)
        for e in range(ELEM_DEV):
            across = []
            for f in range(2):
                valid, row = received(step, 1, e, f)
                across.append(jnp.where(valid, row + back[e][f], 0.0))
            store_row(k + 2, e, add_all(own[e], x_part(e, across)))
        if step == 0:
            make_traces()
            out_x[1, 0, 0] = traces[0]
            out_x[1, 0, 1] = traces[1]
            send_x(1, 0)

    grams[3] = gram_column(basis, 3)
    grams[4] = gram_column(basis, 4)
    packed = jnp.zeros((8, 128), F32)
    for k in range(BASIS):
        packed = pack(packed, k, grams[k])
    message[0] = packed

    def plane_copy(d):
        return pltpu.make_async_remote_copy(
            src_ref=message.at[0],
            dst_ref=got_plane.at[PLANE - d - 1],
            send_sem=p_send,
            recv_sem=p_recv,
            device_id=(plane0 + (place + d) % PLANE,),
            device_id_type=MESH,
        )

    def z_copy(d, to):
        return pltpu.make_async_remote_copy(
            src_ref=message.at[1],
            dst_ref=got_z.at[(N_Z - d) % N_Z],
            send_sem=z_send,
            recv_sem=z_recv,
            device_id=(((z + d) % N_Z) * PLANE + place - core + to,),
            device_id_type=MESH,
        )

    def wait_all(ref, sem):
        pltpu.make_async_copy(ref, ref, sem).wait()

    far_first = sorted(range(1, N_Z), key=lambda d: -min(d, N_Z - d))

    @pl.when(core == 1)
    def _():
        for d in range(2, PLANE, 2):
            plane_copy(d).start()
        wait_all(got_plane, p_recv)
        high, low = sum_messages([message[0]] + [got_plane[i] for i in range(PLANE - 1)])
        message[1] = repack(high, low)
        for d in far_first:
            z_copy(d, 0).start()
        for d in far_first:
            z_copy(d, 1).start()
        z_copy(0, 0).start()
        got_z[0] = message[1]
        wait_all(got_z.at[pl.ds(1, N_Z - 1)], z_recv)

    @pl.when(core == 0)
    def _():
        for d in range(1, PLANE, 2):
            plane_copy(d).start()
        wait_all(got_z, z_recv)

    high, low = sum_messages([got_z[i] for i in range(N_Z)])
    factors, r, inverse, y = solve(high, low)

    sub, lane = iota((8, 128), 0), iota((8, 128), 1)
    r_tile = jnp.zeros((8, 128), F32)
    for (i, k), value in r.items():
        r_tile = jnp.where(jnp.logical_and(sub == i, lane == k), value, r_tile)
    r_ref[...] = r_tile[0:BASIS, 0:BASIS]
    columns = []
    for j in range(BASIS - 1):
        column = jnp.zeros((8, 128), F32)
        for i in range(j + 1, BASIS):
            column = jnp.where(sub == i, factors[i, j], column)
        columns.append(column)
    scale, weight = jnp.zeros((8, 128), F32), jnp.zeros((8, 128), F32)
    for j in range(BASIS):
        scale = jnp.where(sub == j, inverse[j], scale)
        if j < POWERS:
            weight = jnp.where(sub == j, y[j], weight)
    for e in range(ELEM_DEV):
        for t in range(3):
            lanes = min(128, WIDTH - 128 * t)
            x = basis[e, :, 128 * t : 128 * t + 128]
            for j in range(BASIS - 1):
                x = x - columns[j] * x[j : j + 1, :]
            x = x * scale
            q_ref[e, :, 128 * t : 128 * t + lanes] = x[0:BASIS, 0:lanes]
            update = jnp.sum(x * weight, axis=0, keepdims=True)
            up_ref[e : e + 1, 128 * t : 128 * t + lanes] = update[:, 0:lanes]

    for side in range(2):
        @pl.when(me > 0 if side == 0 else me < N_DEV - 1)
        def _():
            far_copy(side).wait_send()
            for step in range(2):
                for kind in range(2):
                    x_copy(step, kind, side).wait_send()

    @pl.when(core == 1)
    def _():
        wait_all(got_plane.at[pl.ds(0, 15)], p_send)
        wait_all(got_plane.at[pl.ds(0, 2 * N_Z - 1)], z_send)

    @pl.when(core == 0)
    def _():
        wait_all(got_plane.at[pl.ds(0, 16)], p_send)


def body(right_side, diag_blocks, face_blocks, neighbours):
    any_space = pl.BlockSpec(memory_space=pl.ANY)
    vmem = pl.BlockSpec(memory_space=pltpu.VMEM)
    tile = (8, 128)
    return pl.pallas_call(
        kernel,
        out_shape=(
            jax.ShapeDtypeStruct((ELEM_DEV, BASIS, WIDTH), F32),
            jax.ShapeDtypeStruct((BASIS, BASIS), F32),
            jax.ShapeDtypeStruct((ELEM_DEV, WIDTH), F32),
        ),
        in_specs=[pl.BlockSpec(memory_space=pltpu.SMEM), vmem, any_space, any_space],
        out_specs=(vmem, vmem, vmem),
        scratch_shapes=[
            pltpu.VMEM((ELEM_DEV, WIDTH, WIDTH), F32),
            pltpu.VMEM((ELEM_DEV, 6, FACE_WIDTH, FACE_WIDTH), F32),
            pltpu.VMEM((ELEM_DEV, 8, 384), F32),
            pltpu.VMEM((8, 384), F32),
            pltpu.VMEM((6,) + tile, F32),
            pltpu.VMEM((2, 2, 2) + tile, F32),
            pltpu.VMEM((2,) + tile, F32),
            pltpu.VMEM((2,) + tile, F32),
            pltpu.VMEM((2,) + tile, F32),
            pltpu.VMEM((2,) + tile, F32),
            pltpu.VMEM((2, ELEM_DEV, FACE_WIDTH, FACE_WIDTH), F32),
            pltpu.VMEM((2,) + tile, F32),
            pltpu.VMEM((PLANE - 1,) + tile, F32),
            pltpu.VMEM((N_Z,) + tile, F32),
            pltpu.SemaphoreType.DMA((2,)),
            pltpu.SemaphoreType.DMA((2,)),
            pltpu.SemaphoreType.DMA((2,)),
            pltpu.SemaphoreType.DMA((2, 2, 2)),
            pltpu.SemaphoreType.DMA((2, 2, 2)),
            pltpu.SemaphoreType.DMA,
            pltpu.SemaphoreType.DMA,
            pltpu.SemaphoreType.DMA,
            pltpu.SemaphoreType.DMA,
        ],
        compiler_params=pltpu.CompilerParams(
            collective_id=0, has_side_effects=True, vmem_limit_bytes=24 * 2**20
        ),
    )(neighbours, right_side, diag_blocks, face_blocks)


def solution(mesh):
    in_specs = (
        P("elem", None),
        P("elem", None, None),
        P("elem", None, None, None),
        P("elem", None),
    )
    out_specs = (P("elem", None, None), P(), P("elem", None))
    return jax.shard_map(body, mesh=mesh, in_specs=in_specs, out_specs=out_specs, check_vma=False)
```

time: 835 us -> 50.3 us (0.06)
  the two profiles are of different devices: /device:TPU:62 before, /device:TPU:1 now
where the time goes in v1:
time: 50.3 us; the launch traced here: 50.1 us
  Pallas kernels  43.5 us (86%)
  local copies, waits for them, and re-layouts  5.92 us (12%)
  between operations  0.65 us (1%)
    pallas_call x1, Pallas kernels, body(): pl.pallas_call(kernel, out_shape=(jax.ShapeDtypeStruct((ELEM_DEV, BASIS,...  43.5 us
    unnamed x10, local copies, waits for them, and re-layouts  5.3 us

profile of v1, /device:TPU:1, one launch (start us, length us, event | category | flops | bytes accessed | tf_op | source)
XLA Modules:
  0.0 50.1 jit_solution(15334615465145212687)
XLA Ops:
  0.6 0.0 copy-start
  0.6 1.5 %copy-done = f32[4,320,320]{2,1,0:T(8,128)S(1)} copy-done((f32[4,320,320]{2,1,0:T(8,128)S(1)}, f32[4,320,320]{2,1,0:T(8,128)}, u32[]{:S(2)}) %copy-start) | copy-done | bytes 1638424
  2.2 0.0 copy-start.1
  2.2 1.2 %copy-done.1 = f32[4,6,80,80]{3,2,1,0:T(8,128)S(1)} copy-done((f32[4,6,80,80]{3,2,1,0:T(8,128)S(1)}, f32[4,6,80,80]{3,2,1,0:T(8,128)}, u32[]{:S(2)}) %copy-start.1) | copy-done | bytes 614424
  3.4 0.0 copy-start.2
  3.4 0.7 %copy-done.2 = f32[4,320]{1,0:T(4,128)S(1)} copy-done((f32[4,320]{1,0:T(4,128)S(1)}, f32[4,320]{1,0:T(4,128)}, u32[]{:S(2)}) %copy-start.2) | copy-done | bytes 5144
  4.1 0.0 copy-start.3
  4.1 0.7 %copy-done.3 = s32[4,6]{1,0:T(4,128)S(1)} copy-done((s32[4,6]{1,0:T(4,128)S(1)}, s32[4,6]{1,0:T(4,128)}, u32[]{:S(2)}) %copy-start.3) | copy-done | bytes 120
  4.8 43.5 %shard_map.67 = (f32[4,5,320]{2,1,0:T(8,128)S(1)}, f32[5,5]{1,0:T(8,128)S(1)}, f32[4,320]{1,0:T(4,128)S(1)}) custom-call(s32[4,6]{1,0:T(4,128)S(1)} %copy-done.3, f32[4,320]{1,0:T(4,128)S(1)} %copy-done.2, f32[4,320,320]{2,1,0:T(8,128)S(1)} %copy-done, f32[4,6,80,80]{3,2,1,0:T(8,128)S(1)} %copy-done.1), custom_call_target="tpu_custom_call" | custom-call | tf_op jit(solution)/shard_map/pallas_call | solution.py:537
  48.3 0.6 %copy.7 = f32[4,5,320]{2,0,1:T(4,128)} copy(f32[4,5,320]{2,1,0:T(8,128)S(1)} %get-tuple-element.3) | data formatting | bytes 51200 | tf_op jit(solution)/shard_map/pallas_call | solution.py:537
  48.9 0.6 %copy.10 = f32[5,5]{1,0:T(8,128)} copy(f32[5,5]{1,0:T(8,128)S(1)} %get-tuple-element.10) | data formatting | bytes 200
  49.5 0.6 %copy.11 = f32[4,320]{1,0:T(4,128)} copy(f32[4,320]{1,0:T(4,128)S(1)} %get-tuple-element.11) | data formatting | bytes 10240
Async XLA Ops:
  0.6 1.5 %copy-start = (f32[4,320,320]{2,1,0:T(8,128)S(1)}, f32[4,320,320]{2,1,0:T(8,128)}, u32[]{:S(2)}) copy-start(f32[4,320,320]{2,1,0:T(8,128)} %diag_hbm.1) | copy-start | bytes 4915204
  2.2 1.2 %copy-start.1 = (f32[4,6,80,80]{3,2,1,0:T(8,128)S(1)}, f32[4,6,80,80]{3,2,1,0:T(8,128)}, u32[]{:S(2)}) copy-start(f32[4,6,80,80]{3,2,1,0:T(8,128)} %face_hbm.1) | copy-start | bytes 1843204
  3.4 0.7 %copy-start.2 = (f32[4,320]{1,0:T(4,128)S(1)}, f32[4,320]{1,0:T(4,128)}, u32[]{:S(2)}) copy-start(f32[4,320]{1,0:T(4,128)} %rhs_ref.1) | copy-start | bytes 15364
  4.1 0.7 %copy-start.3 = (s32[4,6]{1,0:T(4,128)S(1)}, s32[4,6]{1,0:T(4,128)}, u32[]{:S(2)}) copy-start(s32[4,6]{1,0:T(4,128)} %nb_ref.1) | copy-start | bytes 292

commit v2 on v1

--- a/solution.py
+++ b/solution.py
@@ -233,19 +233,25 @@
 
 
 def kernel(
-    nb_ref, rhs_ref, diag_hbm, face_hbm,
-    q_ref, r_ref, up_ref,
-    diag, face, basis, rows, traces, out_x, in_a, in_b, in_c, in_d, far, message, got_plane, got_z,
-    load_sem, far_send, far_recv, x_send, x_recv, p_send, p_recv, z_send, z_recv,
+    nb_hbm, rhs_hbm, diag_hbm, face_hbm,
+    basis_hbm, gram_hbm,
+    nb_ref, rhs_ref, diag, face, basis, gram, rows, traces, out_x, in_a, in_b, in_c, in_d, far, message, got_plane, got_z,
+    load_sem, far_send, far_recv, x_send, x_recv, p_send, p_recv, z_send, z_recv, ready,
 ):
     in_x = ((in_a, in_b), (in_c, in_d))
     me = lax.axis_index("elem")
     place, z, core = me % PLANE, me // PLANE, me % 2
     plane0 = me - place
 
+    stores = [
+        pltpu.make_async_copy(basis, basis_hbm, load_sem.at[4]),
+        pltpu.make_async_copy(gram, gram_hbm, load_sem.at[5]),
+    ]
     loads = [
+        pltpu.make_async_copy(rhs_hbm, rhs_ref, load_sem.at[2]),
         pltpu.make_async_copy(diag_hbm, diag, load_sem.at[0]),
         pltpu.make_async_copy(face_hbm, face, load_sem.at[1]),
+        pltpu.make_async_copy(nb_hbm, nb_ref, load_sem.at[3]),
     ]
     for load in loads:
         load.start()
@@ -255,8 +261,11 @@
     def greet(device):
         pl.semaphore_signal(barrier, inc=1, device_id=(device,), device_id_type=MESH)
 
-    for d in range(1, N_Z):
-        greet(((z + d) % N_Z) * PLANE + place - core + 1)
+    def other_plane(d, to):
+        return ((z + d) % N_Z) * PLANE + place - core + to
+
+    greet(other_plane(1, 1))
+    greet(other_plane(N_Z - 1, 1))
 
     @pl.when(core == 1)
     def _():
@@ -275,8 +284,22 @@
         def _():
             greet(me - 1)
 
+    def tell(reach):
+        @pl.when(core == 1)
+        def _():
+            for d in (reach, N_Z - reach):
+                pl.semaphore_signal(
+                    ready.at[reach // 2], inc=1, device_id=(other_plane(d, 1),), device_id_type=MESH
+                )
+
+    def hear(reach):
+        @pl.when(core == 1)
+        def _():
+            pl.semaphore_wait(ready.at[reach // 2], 2)
+
     basis[...] = jnp.zeros(basis.shape, F32)
     rows[...] = jnp.zeros(rows.shape, F32)
+    loads[0].wait()
     rows[0:ELEM_DEV, 0:WIDTH] = rhs_ref[...]
 
     def store_row(k, e, tiles):
@@ -333,7 +356,7 @@
 
     heard = jnp.where(
         core == 1,
-        (N_Z - 1) * 2 + 15 + 2 - jnp.where(me == N_DEV - 1, 1, 0),
+        4 + 15 + 2 - jnp.where(me == N_DEV - 1, 1, 0),
         16 + jnp.where(jnp.logical_and(place == 0, me > 0), 1, 0),
     )
     pl.semaphore_wait(barrier, heard)
@@ -341,12 +364,14 @@
     out_x[0, 0, 0] = traces[0]
     out_x[0, 0, 1] = traces[1]
     send_x(0, 0)
-    loads[1].wait()
+    tell(1)
+    loads[2].wait()
     for side in range(2):
         @pl.when(me > 0 if side == 0 else me < N_DEV - 1)
         def _():
             far_copy(side).start()
-    loads[0].wait()
+    loads[1].wait()
+    loads[3].wait()
 
     base = me * ELEM_DEV
 
@@ -417,6 +442,8 @@
         own = []
         own_part(own)
         wait_x(step, 1)
+        hear(1 + step)
+        tell(2 + 2 * step)
         for e in range(ELEM_DEV):
             across = []
             for f in range(2):
@@ -429,6 +456,7 @@
             out_x[1, 0, 1] = traces[1]
             send_x(1, 0)
 
+    stores[0].start()
     grams[3] = gram_column(basis, 3)
     grams[4] = gram_column(basis, 4)
     packed = jnp.zeros((8, 128), F32)
@@ -452,7 +480,7 @@
             dst_ref=got_z.at[(N_Z - d) % N_Z],
             send_sem=z_send,
             recv_sem=z_recv,
-            device_id=(((z + d) % N_Z) * PLANE + place - core + to,),
+            device_id=(other_plane(d, to),),
             device_id_type=MESH,
         )
 
@@ -468,6 +496,7 @@
         wait_all(got_plane, p_recv)
         high, low = sum_messages([message[0]] + [got_plane[i] for i in range(PLANE - 1)])
         message[1] = repack(high, low)
+        hear(4)
         for d in far_first:
             z_copy(d, 0).start()
         for d in far_first:
@@ -483,6 +512,45 @@
         wait_all(got_z, z_recv)
 
     high, low = sum_messages([got_z[i] for i in range(N_Z)])
+    gram[0] = high
+    gram[1] = low
+    stores[1].start()
+
+    for side in range(2):
+        @pl.when(me > 0 if side == 0 else me < N_DEV - 1)
+        def _():
+            far_copy(side).wait_send()
+            for step in range(2):
+                for kind in range(2):
+                    x_copy(step, kind, side).wait_send()
+
+    @pl.when(core == 1)
+    def _():
+        wait_all(got_plane.at[pl.ds(0, 15)], p_send)
+        wait_all(got_plane.at[pl.ds(0, 2 * N_Z - 1)], z_send)
+
+    @pl.when(core == 0)
+    def _():
+        wait_all(got_plane.at[pl.ds(0, 16)], p_send)
+
+    for store in stores:
+        store.wait()
+
+
+def finish(basis_hbm, gram_hbm, q_hbm, r_hbm, up_hbm, basis_ref, gram_ref, q_ref, r_ref, up_ref, sem):
+    loads = [
+        pltpu.make_async_copy(gram_hbm, gram_ref, sem.at[0]),
+        pltpu.make_async_copy(basis_hbm, basis_ref, sem.at[1]),
+    ]
+    stores = [
+        pltpu.make_async_copy(q_ref, q_hbm, sem.at[2]),
+        pltpu.make_async_copy(r_ref, r_hbm, sem.at[3]),
+        pltpu.make_async_copy(up_ref, up_hbm, sem.at[4]),
+    ]
+    for load in loads:
+        load.start()
+    loads[0].wait()
+    high, low = gram_ref[0], gram_ref[1]
     factors, r, inverse, y = solve(high, low)
 
     sub, lane = iota((8, 128), 0), iota((8, 128), 1)
@@ -490,6 +558,7 @@
     for (i, k), value in r.items():
         r_tile = jnp.where(jnp.logical_and(sub == i, lane == k), value, r_tile)
     r_ref[...] = r_tile[0:BASIS, 0:BASIS]
+    stores[1].start()
     columns = []
     for j in range(BASIS - 1):
         column = jnp.zeros((8, 128), F32)
@@ -501,52 +570,41 @@
         scale = jnp.where(sub == j, inverse[j], scale)
         if j < POWERS:
             weight = jnp.where(sub == j, y[j], weight)
+    loads[1].wait()
     for e in range(ELEM_DEV):
         for t in range(3):
             lanes = min(128, WIDTH - 128 * t)
-            x = basis[e, :, 128 * t : 128 * t + 128]
+            x = basis_ref[e, :, 128 * t : 128 * t + 128]
             for j in range(BASIS - 1):
                 x = x - columns[j] * x[j : j + 1, :]
             x = x * scale
-            q_ref[e, :, 128 * t : 128 * t + lanes] = x[0:BASIS, 0:lanes]
+            q_ref[:, e, 128 * t : 128 * t + lanes] = x[0:BASIS, 0:lanes]
             update = jnp.sum(x * weight, axis=0, keepdims=True)
             up_ref[e : e + 1, 128 * t : 128 * t + lanes] = update[:, 0:lanes]
-
-    for side in range(2):
-        @pl.when(me > 0 if side == 0 else me < N_DEV - 1)
-        def _():
-            far_copy(side).wait_send()
-            for step in range(2):
-                for kind in range(2):
-                    x_copy(step, kind, side).wait_send()
-
-    @pl.when(core == 1)
-    def _():
-        wait_all(got_plane.at[pl.ds(0, 15)], p_send)
-        wait_all(got_plane.at[pl.ds(0, 2 * N_Z - 1)], z_send)
-
-    @pl.when(core == 0)
-    def _():
-        wait_all(got_plane.at[pl.ds(0, 16)], p_send)
+    stores[0].start()
+    stores[2].start()
+    for store in stores:
+        store.wait()
 
 
 def body(right_side, diag_blocks, face_blocks, neighbours):
-    any_space = pl.BlockSpec(memory_space=pl.ANY)
-    vmem = pl.BlockSpec(memory_space=pltpu.VMEM)
+    hbm = pl.BlockSpec(memory_space=pl.ANY)
     tile = (8, 128)
-    return pl.pallas_call(
+    basis, gram = pl.pallas_call(
         kernel,
         out_shape=(
-            jax.ShapeDtypeStruct((ELEM_DEV, BASIS, WIDTH), F32),
-            jax.ShapeDtypeStruct((BASIS, BASIS), F32),
-            jax.ShapeDtypeStruct((ELEM_DEV, WIDTH), F32),
+            jax.ShapeDtypeStruct((ELEM_DEV, 8, 384), F32),
+            jax.ShapeDtypeStruct((2,) + tile, F32),
         ),
-        in_specs=[pl.BlockSpec(memory_space=pltpu.SMEM), vmem, any_space, any_space],
-        out_specs=(vmem, vmem, vmem),
+        in_specs=[hbm] * 4,
+        out_specs=(hbm, hbm),
         scratch_shapes=[
+            pltpu.SMEM((ELEM_DEV, 6), jnp.int32),
+            pltpu.VMEM((ELEM_DEV, WIDTH), F32),
             pltpu.VMEM((ELEM_DEV, WIDTH, WIDTH), F32),
             pltpu.VMEM((ELEM_DEV, 6, FACE_WIDTH, FACE_WIDTH), F32),
             pltpu.VMEM((ELEM_DEV, 8, 384), F32),
+            pltpu.VMEM((2,) + tile, F32),
             pltpu.VMEM((8, 384), F32),
             pltpu.VMEM((6,) + tile, F32),
             pltpu.VMEM((2, 2, 2) + tile, F32),
@@ -558,7 +616,7 @@
             pltpu.VMEM((2,) + tile, F32),
             pltpu.VMEM((PLANE - 1,) + tile, F32),
             pltpu.VMEM((N_Z,) + tile, F32),
-            pltpu.SemaphoreType.DMA((2,)),
+            pltpu.SemaphoreType.DMA((6,)),
             pltpu.SemaphoreType.DMA((2,)),
             pltpu.SemaphoreType.DMA((2,)),
             pltpu.SemaphoreType.DMA((2, 2, 2)),
@@ -567,11 +625,32 @@
             pltpu.SemaphoreType.DMA,
             pltpu.SemaphoreType.DMA,
             pltpu.SemaphoreType.DMA,
+            pltpu.SemaphoreType.REGULAR((3,)),
         ],
         compiler_params=pltpu.CompilerParams(
-            collective_id=0, has_side_effects=True, vmem_limit_bytes=24 * 2**20
+            collective_id=0, has_side_effects=True, vmem_limit_bytes=62 * 2**20
         ),
     )(neighbours, right_side, diag_blocks, face_blocks)
+    basis_q, r_factor, update = pl.pallas_call(
+        finish,
+        out_shape=(
+            jax.ShapeDtypeStruct((BASIS, ELEM_DEV, WIDTH), F32),
+            jax.ShapeDtypeStruct((BASIS, BASIS), F32),
+            jax.ShapeDtypeStruct((ELEM_DEV, WIDTH), F32),
+        ),
+        in_specs=[hbm, hbm],
+        out_specs=(hbm, hbm, hbm),
+        scratch_shapes=[
+            pltpu.VMEM((ELEM_DEV, 8, 384), F32),
+            pltpu.VMEM((2,) + tile, F32),
+            pltpu.VMEM((BASIS, ELEM_DEV, WIDTH), F32),
+            pltpu.VMEM((BASIS, BASIS), F32),
+            pltpu.VMEM((ELEM_DEV, WIDTH), F32),
+            pltpu.SemaphoreType.DMA((5,)),
+        ],
+        compiler_params=pltpu.CompilerParams(vmem_limit_bytes=62 * 2**20),
+    )(basis, gram)
+    return basis_q.transpose(1, 0, 2), r_factor, update
 
 
 def solution(mesh):

time: 50.3 us -> 42.7 us (0.85)
  local copies, waits for them, and re-layouts: 5.92 us -> 0 us
  Pallas kernels: 43.5 us -> 41.8 us
    unnamed x10 -> x0, local copies, waits for them, and re-layouts: 5.3 us -> none
    pallas_call x1 -> x2, Pallas kernels: 43.5 us -> 41.8 us  [the longest x1 40.1 us: body(): pl.pallas_call(kernel, out_shape=(jax.ShapeDtypeStruct((ELEM_DEV, 8, 384)...]
    pallas_call x1 -> x0, local copies, waits for them, and re-layouts: 0.62 us -> none  [body(): pl.pallas_call(kernel, out_shape=(jax.ShapeDtypeStruct((ELEM_DEV, BASIS,...]
where the time goes in v2:
time: 42.7 us; the launch traced here: 42.5 us
  Pallas kernels  41.8 us (98%)
  between operations  0.64 us (1%)
    pallas_call x1, Pallas kernels, body(): pl.pallas_call(kernel, out_shape=(jax.ShapeDtypeStruct((ELEM_DEV, 8, 384)...  40.1 us
    pallas_call x1, Pallas kernels, body(): pl.pallas_call(finish, out_shape=(jax.ShapeDtypeStruct((BASIS, ELEM_DEV,...  1.68 us

profile of v2, /device:TPU:1, one launch (start us, length us, event | category | flops | bytes accessed | tf_op | source)
XLA Modules:
  0.0 42.5 jit_solution(11971305149456800849)
XLA Ops:
  0.6 40.1 %shard_map.67 = (f32[4,8,384]{2,1,0:T(8,128)}, f32[2,8,128]{2,1,0:T(8,128)}) custom-call(s32[4,6]{1,0:T(4,128)} %nb_hbm.1, f32[4,320]{1,0:T(4,128)} %rhs_hbm.1, f32[4,320,320]{2,1,0:T(8,128)} %diag_hbm.1, f32[4,6,80,80]{3,2,1,0:T(8,128)} %face_hbm.1), custom_call_target="tpu_custom_call" | custom-call | tf_op jit(solution)/shard_map/pallas_call | solution.py:593
  40.8 1.7 %shard_map.68 = (f32[5,4,320]{2,1,0:T(4,128)}, f32[5,5]{1,0:T(8,128)}, f32[4,320]{1,0:T(4,128)}) custom-call(f32[4,8,384]{2,1,0:T(8,128)} %get-tuple-element.8.basis_hbm, f32[2,8,128]{2,1,0:T(8,128)} %get-tuple-element.9.gram_hbm), custom_call_target="tpu_custom_call" | custom-call | tf_op jit(solution)/shard_map/pallas_call | solution.py:634

commit v3 on v2

--- a/solution.py
+++ b/solution.py
@@ -134,11 +134,10 @@
     for other, other_low in chains[1:]:
         total, more = two_sum(total, other)
         low = low + (other_low + more)
-    for shift in (64, 32, 16, 8, 4, 2, 1):
-        other, other_low = pltpu.roll(total, shift, 1), pltpu.roll(low, shift, 1)
-        total, more = two_sum(total, other)
-        low = (low + other_low) + more
-    return total, low
+    grid = jnp.minimum(256.0 * jnp.max(jnp.abs(total), axis=1, keepdims=True), 1e38)
+    lead = (total + grid) - grid
+    rest = (total - lead) + low
+    return jnp.sum(lead, axis=1, keepdims=True), jnp.sum(rest, axis=1, keepdims=True)
 
 
 def pack(message, k, pair):
@@ -149,8 +148,8 @@
 
 def sum_messages(tiles):
     chains = []
-    for start in range(4):
-        mine = tiles[start::4]
+    for start in range(8):
+        mine = tiles[start::8]
         total, low = mine[0], jnp.zeros((8, 128), F32)
         for tile in mine[1:]:
             total, more = two_sum(total, tile)
@@ -235,7 +234,7 @@
 def kernel(
     nb_hbm, rhs_hbm, diag_hbm, face_hbm,
     basis_hbm, gram_hbm,
-    nb_ref, rhs_ref, diag, face, basis, gram, rows, traces, out_x, in_a, in_b, in_c, in_d, far, message, got_plane, got_z,
+    nb_ref, rhs_ref, diag, face, basis, gram, rows, traces, out_x, in_a, in_b, in_c, in_d, packed_face, far, message, got_plane, got_z,
     load_sem, far_send, far_recv, x_send, x_recv, p_send, p_recv, z_send, z_recv, ready,
 ):
     in_x = ((in_a, in_b), (in_c, in_d))
@@ -264,25 +263,28 @@
     def other_plane(d, to):
         return ((z + d) % N_Z) * PLANE + place - core + to
 
-    greet(other_plane(1, 1))
-    greet(other_plane(N_Z - 1, 1))
-
     @pl.when(core == 1)
     def _():
-        for d in range(1, PLANE):
-            greet(plane0 + (place + d) % PLANE)
+        greet(plane0 + (place + PLANE - 1) % PLANE)
+        greet(plane0 + (place + 1) % PLANE)
 
         @pl.when(jnp.logical_and(place == PLANE - 1, me < N_DEV - 1))
         def _():
             greet(me + 1)
 
+        for d in range(2, PLANE - 1):
+            greet(plane0 + (place + d) % PLANE)
+
     @pl.when(core == 0)
     def _():
-        greet(me + 1)
-
         @pl.when(me > 0)
         def _():
             greet(me - 1)
+
+        greet(me + 1)
+
+    greet(other_plane(1, 1))
+    greet(other_plane(N_Z - 1, 1))
 
     def tell(reach):
         @pl.when(core == 1)
@@ -346,30 +348,25 @@
 
     def far_copy(side):
         return pltpu.make_async_remote_copy(
-            src_ref=face.at[:, side],
-            dst_ref=far.at[1 - side],
+            src_ref=packed_face.at[side],
+            dst_ref=far.at[1 - side, pl.ds(0, 3)],
             send_sem=far_send.at[side],
             recv_sem=far_recv.at[1 - side],
             device_id=(me - 1 if side == 0 else me + 1,),
             device_id_type=MESH,
         )
 
-    heard = jnp.where(
-        core == 1,
-        4 + 15 + 2 - jnp.where(me == N_DEV - 1, 1, 0),
-        16 + jnp.where(jnp.logical_and(place == 0, me > 0), 1, 0),
-    )
-    pl.semaphore_wait(barrier, heard)
-
     out_x[0, 0, 0] = traces[0]
     out_x[0, 0, 1] = traces[1]
-    send_x(0, 0)
-    tell(1)
     loads[2].wait()
     for side in range(2):
-        @pl.when(me > 0 if side == 0 else me < N_DEV - 1)
-        def _():
-            far_copy(side).start()
+        packed_face[side, 2, :, FACE_WIDTH:128] = jnp.zeros((FACE_WIDTH, 48), F32)
+        for b in range(3):
+            packed_face[side, b, :, 0:FACE_WIDTH] = face[b, side]
+        packed_face[side, 0, :, FACE_WIDTH:128] = face[3, side, :, 0:48]
+        packed_face[side, 1, :, FACE_WIDTH:128] = jnp.concatenate(
+            [face[3, side, :, 48:FACE_WIDTH], jnp.zeros((FACE_WIDTH, 16), F32)], axis=1
+        )
     loads[1].wait()
     loads[3].wait()
 
@@ -402,6 +399,11 @@
         valid, index = links[e][f]
         return valid, in_x[step][kind][f, pl.ds(index, 1), :]
 
+    heard = jnp.where(
+        core == 1,
+        4 + 15 + 2 - jnp.where(me == N_DEV - 1, 1, 0),
+        16 + jnp.where(jnp.logical_and(place == 0, me > 0), 1, 0),
+    )
     grams = {}
     for step in range(2):
         k = 2 * step
@@ -414,20 +416,24 @@
         low, high = x_traces(sums)
         out_x[step, 1, 0] = low
         out_x[step, 1, 1] = high
-        send_x(step, 1)
         if step == 0:
+            pl.semaphore_wait(barrier, heard)
+            send_x(0, 0)
+            send_x(0, 1)
             for side in range(2):
-                @pl.when(me < N_DEV - 1 if side == 0 else me > 0)
+                @pl.when(me > 0 if side == 0 else me < N_DEV - 1)
                 def _():
-                    far_copy(side).wait_recv()
-        back = []
-        for e in range(ELEM_DEV):
-            pair = []
-            for f in range(2):
-                valid, index = links[e][f]
-                trace = traces[f, e : e + 1, 0:FACE_WIDTH]
-                pair.append(place_trace(matvec(far[f, index], trace)))
-            back.append(pair)
+                    far_copy(side).start()
+            tell(1)
+        else:
+            send_x(step, 1)
+        kept = [[traces[f, e : e + 1, 0:FACE_WIDTH] for f in range(2)] for e in range(ELEM_DEV)]
+
+        def added(e, f):
+            return place_trace(matvec(far[f, links[e][f][1], :, 0:FACE_WIDTH], kept[e][f]))
+
+        if step == 1:
+            back = [[added(e, f) for f in range(2)] for e in range(ELEM_DEV)]
         if step == 1:
             for kk in range(3):
                 grams[kk] = gram_column(basis, kk)
@@ -442,6 +448,15 @@
         own = []
         own_part(own)
         wait_x(step, 1)
+        if step == 0:
+            for side in range(2):
+                @pl.when(me < N_DEV - 1 if side == 0 else me > 0)
+                def _():
+                    far_copy(side).wait_recv()
+                head = far[1 - side, 0:2, :, FACE_WIDTH:128]
+                far[1 - side, 3, :, 0:48] = head[0]
+                far[1 - side, 3, :, 48:FACE_WIDTH] = head[1, :, 0:32]
+            back = [[added(e, f) for f in range(2)] for e in range(ELEM_DEV)]
         hear(1 + step)
         tell(2 + 2 * step)
         for e in range(ELEM_DEV):
@@ -499,7 +514,6 @@
         hear(4)
         for d in far_first:
             z_copy(d, 0).start()
-        for d in far_first:
             z_copy(d, 1).start()
         z_copy(0, 0).start()
         got_z[0] = message[1]
@@ -612,7 +626,8 @@
             pltpu.VMEM((2,) + tile, F32),
             pltpu.VMEM((2,) + tile, F32),
             pltpu.VMEM((2,) + tile, F32),
-            pltpu.VMEM((2, ELEM_DEV, FACE_WIDTH, FACE_WIDTH), F32),
+            pltpu.VMEM((2, 3, FACE_WIDTH, 128), F32),
+            pltpu.VMEM((2, ELEM_DEV, FACE_WIDTH, 128), F32),
             pltpu.VMEM((2,) + tile, F32),
             pltpu.VMEM((PLANE - 1,) + tile, F32),
             pltpu.VMEM((N_Z,) + tile, F32),

time: 42.7 us -> 41.4 us (0.970)
  Pallas kernels: 41.8 us -> 40.5 us
    pallas_call x1, Pallas kernels: 40.1 us -> 38.9 us  [body(): pl.pallas_call(kernel, out_shape=(jax.ShapeDtypeStruct((ELEM_DEV, 8, 384)...]
where the time goes in v3:
time: 41.4 us; the launch traced here: 41.2 us
  Pallas kernels  40.5 us (98%)
  between operations  0.64 us (2%)
    pallas_call x1, Pallas kernels, body(): pl.pallas_call(kernel, out_shape=(jax.ShapeDtypeStruct((ELEM_DEV, 8, 384)...  38.9 us
    pallas_call x1, Pallas kernels, body(): pl.pallas_call(finish, out_shape=(jax.ShapeDtypeStruct((BASIS, ELEM_DEV,...  1.68 us

profile of v3, /device:TPU:1, one launch (start us, length us, event | category | flops | bytes accessed | tf_op | source)
XLA Modules:
  0.0 41.2 jit_solution(7152038529326878352)
XLA Ops:
  0.6 38.9 %shard_map.67 = (f32[4,8,384]{2,1,0:T(8,128)}, f32[2,8,128]{2,1,0:T(8,128)}) custom-call(s32[4,6]{1,0:T(4,128)} %nb_hbm.1, f32[4,320]{1,0:T(4,128)} %rhs_hbm.1, f32[4,320,320]{2,1,0:T(8,128)} %diag_hbm.1, f32[4,6,80,80]{3,2,1,0:T(8,128)} %face_hbm.1), custom_call_target="tpu_custom_call" | custom-call | tf_op jit(solution)/shard_map/pallas_call | solution.py:607
  39.5 1.7 %shard_map.68 = (f32[5,4,320]{2,1,0:T(4,128)}, f32[5,5]{1,0:T(8,128)}, f32[4,320]{1,0:T(4,128)}) custom-call(f32[4,8,384]{2,1,0:T(8,128)} %get-tuple-element.8.basis_hbm, f32[2,8,128]{2,1,0:T(8,128)} %get-tuple-element.9.gram_hbm), custom_call_target="tpu_custom_call" | custom-call | tf_op jit(solution)/shard_map/pallas_call | solution.py:649

commit v4 on v3

--- a/solution.py
+++ b/solution.py
@@ -233,8 +233,8 @@
 
 def kernel(
     nb_hbm, rhs_hbm, diag_hbm, face_hbm,
-    basis_hbm, gram_hbm,
-    nb_ref, rhs_ref, diag, face, basis, gram, rows, traces, out_x, in_a, in_b, in_c, in_d, packed_face, far, message, got_plane, got_z,
+    basis, gram,
+    nb_ref, rhs_ref, diag, face, rows, traces, out_x, in_a, in_b, in_c, in_d, packed_face, far, message, got_plane, got_z,
     load_sem, far_send, far_recv, x_send, x_recv, p_send, p_recv, z_send, z_recv, ready,
 ):
     in_x = ((in_a, in_b), (in_c, in_d))
@@ -242,10 +242,6 @@
     place, z, core = me % PLANE, me // PLANE, me % 2
     plane0 = me - place
 
-    stores = [
-        pltpu.make_async_copy(basis, basis_hbm, load_sem.at[4]),
-        pltpu.make_async_copy(gram, gram_hbm, load_sem.at[5]),
-    ]
     loads = [
         pltpu.make_async_copy(rhs_hbm, rhs_ref, load_sem.at[2]),
         pltpu.make_async_copy(diag_hbm, diag, load_sem.at[0]),
@@ -471,7 +467,6 @@
             out_x[1, 0, 1] = traces[1]
             send_x(1, 0)
 
-    stores[0].start()
     grams[3] = gram_column(basis, 3)
     grams[4] = gram_column(basis, 4)
     packed = jnp.zeros((8, 128), F32)
@@ -528,7 +523,6 @@
     high, low = sum_messages([got_z[i] for i in range(N_Z)])
     gram[0] = high
     gram[1] = low
-    stores[1].start()
 
     for side in range(2):
         @pl.when(me > 0 if side == 0 else me < N_DEV - 1)
@@ -547,23 +541,13 @@
     def _():
         wait_all(got_plane.at[pl.ds(0, 16)], p_send)
 
-    for store in stores:
-        store.wait()
-
-
-def finish(basis_hbm, gram_hbm, q_hbm, r_hbm, up_hbm, basis_ref, gram_ref, q_ref, r_ref, up_ref, sem):
-    loads = [
-        pltpu.make_async_copy(gram_hbm, gram_ref, sem.at[0]),
-        pltpu.make_async_copy(basis_hbm, basis_ref, sem.at[1]),
+
+def finish(basis_ref, gram_ref, q_hbm, r_hbm, up_hbm, q_ref, r_ref, up_ref, sem):
+    stores = [
+        pltpu.make_async_copy(q_ref, q_hbm, sem.at[0]),
+        pltpu.make_async_copy(r_ref, r_hbm, sem.at[1]),
+        pltpu.make_async_copy(up_ref, up_hbm, sem.at[2]),
     ]
-    stores = [
-        pltpu.make_async_copy(q_ref, q_hbm, sem.at[2]),
-        pltpu.make_async_copy(r_ref, r_hbm, sem.at[3]),
-        pltpu.make_async_copy(up_ref, up_hbm, sem.at[4]),
-    ]
-    for load in loads:
-        load.start()
-    loads[0].wait()
     high, low = gram_ref[0], gram_ref[1]
     factors, r, inverse, y = solve(high, low)
 
@@ -584,7 +568,6 @@
         scale = jnp.where(sub == j, inverse[j], scale)
         if j < POWERS:
             weight = jnp.where(sub == j, y[j], weight)
-    loads[1].wait()
     for e in range(ELEM_DEV):
         for t in range(3):
             lanes = min(128, WIDTH - 128 * t)
@@ -603,22 +586,25 @@
 
 def body(right_side, diag_blocks, face_blocks, neighbours):
     hbm = pl.BlockSpec(memory_space=pl.ANY)
+    vmem = pl.BlockSpec(memory_space=pltpu.VMEM)
     tile = (8, 128)
+    operands = [
+        pltpu.with_memory_space_constraint(x, pltpu.HBM)
+        for x in (neighbours, right_side, diag_blocks, face_blocks)
+    ]
     basis, gram = pl.pallas_call(
         kernel,
         out_shape=(
-            jax.ShapeDtypeStruct((ELEM_DEV, 8, 384), F32),
-            jax.ShapeDtypeStruct((2,) + tile, F32),
+            pltpu.VMEM((ELEM_DEV, 8, 384), F32),
+            pltpu.VMEM((2,) + tile, F32),
         ),
         in_specs=[hbm] * 4,
-        out_specs=(hbm, hbm),
+        out_specs=(vmem, vmem),
         scratch_shapes=[
             pltpu.SMEM((ELEM_DEV, 6), jnp.int32),
             pltpu.VMEM((ELEM_DEV, WIDTH), F32),
             pltpu.VMEM((ELEM_DEV, WIDTH, WIDTH), F32),
             pltpu.VMEM((ELEM_DEV, 6, FACE_WIDTH, FACE_WIDTH), F32),
-            pltpu.VMEM((ELEM_DEV, 8, 384), F32),
-            pltpu.VMEM((2,) + tile, F32),
             pltpu.VMEM((8, 384), F32),
             pltpu.VMEM((6,) + tile, F32),
             pltpu.VMEM((2, 2, 2) + tile, F32),
@@ -631,7 +617,7 @@
             pltpu.VMEM((2,) + tile, F32),
             pltpu.VMEM((PLANE - 1,) + tile, F32),
             pltpu.VMEM((N_Z,) + tile, F32),
-            pltpu.SemaphoreType.DMA((6,)),
+            pltpu.SemaphoreType.DMA((4,)),
             pltpu.SemaphoreType.DMA((2,)),
             pltpu.SemaphoreType.DMA((2,)),
             pltpu.SemaphoreType.DMA((2, 2, 2)),
@@ -643,9 +629,9 @@
             pltpu.SemaphoreType.REGULAR((3,)),
         ],
         compiler_params=pltpu.CompilerParams(
-            collective_id=0, has_side_effects=True, vmem_limit_bytes=62 * 2**20
+            collective_id=0, has_side_effects=True, vmem_limit_bytes=24 * 2**20
         ),
-    )(neighbours, right_side, diag_blocks, face_blocks)
+    )(*operands)
     basis_q, r_factor, update = pl.pallas_call(
         finish,
         out_shape=(
@@ -653,17 +639,15 @@
             jax.ShapeDtypeStruct((BASIS, BASIS), F32),
             jax.ShapeDtypeStruct((ELEM_DEV, WIDTH), F32),
         ),
-        in_specs=[hbm, hbm],
+        in_specs=[vmem, vmem],
         out_specs=(hbm, hbm, hbm),
         scratch_shapes=[
-            pltpu.VMEM((ELEM_DEV, 8, 384), F32),
-            pltpu.VMEM((2,) + tile, F32),
             pltpu.VMEM((BASIS, ELEM_DEV, WIDTH), F32),
             pltpu.VMEM((BASIS, BASIS), F32),
             pltpu.VMEM((ELEM_DEV, WIDTH), F32),
-            pltpu.SemaphoreType.DMA((5,)),
+            pltpu.SemaphoreType.DMA((3,)),
         ],
-        compiler_params=pltpu.CompilerParams(vmem_limit_bytes=62 * 2**20),
+        compiler_params=pltpu.CompilerParams(vmem_limit_bytes=4 * 2**20),
     )(basis, gram)
     return basis_q.transpose(1, 0, 2), r_factor, update
 

time: 41.4 us -> 39.8 us (0.961)
  Pallas kernels: 40.5 us -> 39 us
    pallas_call x1, Pallas kernels: 38.9 us -> 38.1 us  [body(): pl.pallas_call(kernel, out_shape=(pltpu.VMEM((ELEM_DEV, 8, 384), F32), pl...]
    pallas_call x1, Pallas kernels: 1.68 us -> 0.94 us  [body(): pl.pallas_call(finish, out_shape=(jax.ShapeDtypeStruct((BASIS, ELEM_DEV,...]
where the time goes in v4:
time: 39.8 us; the launch traced here: 39.7 us
  Pallas kernels  39 us (98%)
  between operations  0.64 us (2%)
    pallas_call x1, Pallas kernels, body(): pl.pallas_call(kernel, out_shape=(pltpu.VMEM((ELEM_DEV, 8, 384), F32), pl...  38.1 us
    pallas_call x1, Pallas kernels, body(): pl.pallas_call(finish, out_shape=(jax.ShapeDtypeStruct((BASIS, ELEM_DEV,...  0.94 us

profile of v4, /device:TPU:1, one launch (start us, length us, event | category | flops | bytes accessed | tf_op | source)
XLA Modules:
  0.0 39.7 jit_solution(12588352138278888646)
XLA Ops:
  0.6 38.1 %shard_map.67 = (f32[4,8,384]{2,1,0:T(8,128)S(1)}, f32[2,8,128]{2,1,0:T(8,128)S(1)}) custom-call(s32[4,6]{1,0:T(4,128)} %nb_hbm.1, f32[4,320]{1,0:T(4,128)} %rhs_hbm.1, f32[4,320,320]{2,1,0:T(8,128)} %diag_hbm.1, f32[4,6,80,80]{3,2,1,0:T(8,128)} %face_hbm.1), custom_call_target="tpu_custom_call" | custom-call | tf_op jit(solution)/shard_map/pallas_call | solution.py:595
  38.7 0.9 %shard_map.68 = (f32[5,4,320]{2,1,0:T(4,128)}, f32[5,5]{1,0:T(8,128)}, f32[4,320]{1,0:T(4,128)}) custom-call(f32[4,8,384]{2,1,0:T(8,128)S(1)} %get-tuple-element.8.basis_ref, f32[2,8,128]{2,1,0:T(8,128)S(1)} %get-tuple-element.9.gram_ref), custom_call_target="tpu_custom_call" | custom-call | tf_op jit(solution)/shard_map/pallas_call | solution.py:635

commit v5 on v4

--- a/solution.py
+++ b/solution.py
@@ -114,6 +114,18 @@
 
 def matvec(matrix, row):
     return jnp.sum(matrix * row, axis=1, keepdims=True)
+
+
+def own_column(diag, face_y, face_z, row, across):
+    part = diag[:, 0:128] * row[:, 0:128] + diag[:, 128:256] * row[:, 128:256]
+    last = diag[:, 256:WIDTH] * row[:, 256:WIDTH]
+    part = part + jnp.concatenate([last, jnp.zeros((WIDTH, 384 - WIDTH), F32)], axis=1)
+    sub = iota((8, 128), 0) % 4
+    both_z = jnp.where(sub == 0, across[4], jnp.where(sub == 3, across[5], 0.0))
+    both_y = jnp.concatenate([jnp.broadcast_to(across[f], (8, 128)) for f in (2, 3)], axis=0)
+    from_z = (face_z.reshape(40, 8, 128) * both_z[None]).reshape(WIDTH, 128)
+    from_y = (face_y.reshape(20, 16, 128) * both_y[None]).reshape(WIDTH, 128)
+    return jnp.sum(part + (from_z + from_y), axis=1, keepdims=True)
 
 
 def gram_column(basis, k):
@@ -234,7 +246,7 @@
 def kernel(
     nb_hbm, rhs_hbm, diag_hbm, face_hbm,
     basis, gram,
-    nb_ref, rhs_ref, diag, face, rows, traces, out_x, in_a, in_b, in_c, in_d, packed_face, far, message, got_plane, got_z,
+    nb_ref, rhs_ref, diag, face, face_y, face_z, rows, traces, out_x, in_a, in_b, in_c, in_d, packed_face, far, message, got_plane, got_z,
     load_sem, far_send, far_recv, x_send, x_recv, p_send, p_recv, z_send, z_recv, ready,
 ):
     in_x = ((in_a, in_b), (in_c, in_d))
@@ -248,9 +260,6 @@
         pltpu.make_async_copy(face_hbm, face, load_sem.at[1]),
         pltpu.make_async_copy(nb_hbm, nb_ref, load_sem.at[3]),
     ]
-    for load in loads:
-        load.start()
-
     barrier = pltpu.get_barrier_semaphore()
 
     def greet(device):
@@ -267,9 +276,6 @@
         @pl.when(jnp.logical_and(place == PLANE - 1, me < N_DEV - 1))
         def _():
             greet(me + 1)
-
-        for d in range(2, PLANE - 1):
-            greet(plane0 + (place + d) % PLANE)
 
     @pl.when(core == 0)
     def _():
@@ -278,6 +284,14 @@
             greet(me - 1)
 
         greet(me + 1)
+
+    for load in loads:
+        load.start()
+
+    @pl.when(core == 1)
+    def _():
+        for d in range(2, PLANE - 1):
+            greet(plane0 + (place + d) % PLANE)
 
     greet(other_plane(1, 1))
     greet(other_plane(N_Z - 1, 1))
@@ -296,6 +310,8 @@
             pl.semaphore_wait(ready.at[reach // 2], 2)
 
     basis[...] = jnp.zeros(basis.shape, F32)
+    face_y[...] = jnp.zeros(face_y.shape, F32)
+    face_z[...] = jnp.zeros(face_z.shape, F32)
     rows[...] = jnp.zeros(rows.shape, F32)
     loads[0].wait()
     rows[0:ELEM_DEV, 0:WIDTH] = rhs_ref[...]
@@ -363,6 +379,14 @@
         packed_face[side, 1, :, FACE_WIDTH:128] = jnp.concatenate(
             [face[3, side, :, 48:FACE_WIDTH], jnp.zeros((FACE_WIDTH, 16), F32)], axis=1
         )
+    for e in range(ELEM_DEV):
+        for c in range(20):
+            face_y[e, 16 * c : 16 * c + 4, 0:FACE_WIDTH] = face[e, 2, 4 * c : 4 * c + 4, :]
+            face_y[e, 16 * c + 12 : 16 * c + 16, 0:FACE_WIDTH] = face[e, 3, 4 * c : 4 * c + 4, :]
+        for f, k in ((4, 0), (5, 3)):
+            face_z[e, pl.ds(k, FACE_WIDTH, stride=4), :] = jnp.concatenate(
+                [face[e, f], jnp.zeros((FACE_WIDTH, 128 - FACE_WIDTH), F32)], axis=1
+            )
     loads[1].wait()
     loads[3].wait()
 
@@ -377,12 +401,11 @@
 
     def own_part(out):
         for e in range(ELEM_DEV):
-            total = place_element(matvec(diag[e], rows[e : e + 1, 0:WIDTH]))
+            across = {}
             for f in range(2, 6):
                 valid, index = links[e][f]
-                row = jnp.where(valid, traces[f ^ 1, pl.ds(index, 1), :], 0.0)
-                total = add_all(total, place_face(f, matvec(face[e, f], row[:, 0:FACE_WIDTH])))
-            out.append(total)
+                across[f] = jnp.where(valid, traces[f ^ 1, pl.ds(index, 1), :], 0.0)
+            out.append(place_element(own_column(diag[e], face_y[e], face_z[e], rows[e : e + 1, :], across)))
 
     def x_part(e, across):
         total = None
@@ -434,6 +457,8 @@
             for kk in range(3):
                 grams[kk] = gram_column(basis, kk)
         wait_x(step, 0)
+        hear(1 + step)
+        tell(2 + 2 * step)
         for e in range(ELEM_DEV):
             across = []
             for f in range(2):
@@ -453,8 +478,6 @@
                 far[1 - side, 3, :, 0:48] = head[0]
                 far[1 - side, 3, :, 48:FACE_WIDTH] = head[1, :, 0:32]
             back = [[added(e, f) for f in range(2)] for e in range(ELEM_DEV)]
-        hear(1 + step)
-        tell(2 + 2 * step)
         for e in range(ELEM_DEV):
             across = []
             for f in range(2):
@@ -484,43 +507,47 @@
             device_id_type=MESH,
         )
 
-    def z_copy(d, to):
+    def z_copy(source, plane, to, same):
         return pltpu.make_async_remote_copy(
-            src_ref=message.at[1],
-            dst_ref=got_z.at[(N_Z - d) % N_Z],
+            src_ref=message.at[source],
+            dst_ref=got_z.at[(z - plane + N_Z) % N_Z + (0 if same else N_Z)],
             send_sem=z_send,
             recv_sem=z_recv,
-            device_id=(other_plane(d, to),),
+            device_id=(plane * PLANE + place - core + to,),
             device_id_type=MESH,
         )
 
+    def send_z(source, mine):
+        for i in range(N_Z - 1):
+            plane = i + jnp.where(z <= i, 1, 0)
+            z_copy(source, plane, 1, mine == 1).start()
+            z_copy(source, plane, 0, mine == 0).start()
+        z_copy(source, z, 1 - mine, False).start()
+        got_z[0] = message[source]
+
     def wait_all(ref, sem):
         pltpu.make_async_copy(ref, ref, sem).wait()
-
-    far_first = sorted(range(1, N_Z), key=lambda d: -min(d, N_Z - d))
 
     @pl.when(core == 1)
     def _():
         for d in range(2, PLANE, 2):
             plane_copy(d).start()
+        hear(4)
+        pl.semaphore_signal(ready.at[3], inc=1, device_id=(me - 1,), device_id_type=MESH)
         wait_all(got_plane, p_recv)
-        high, low = sum_messages([message[0]] + [got_plane[i] for i in range(PLANE - 1)])
+        high, low = sum_messages([message[0]] + [got_plane[i] for i in range(PLANE - 2)])
         message[1] = repack(high, low)
-        hear(4)
-        for d in far_first:
-            z_copy(d, 0).start()
-            z_copy(d, 1).start()
-        z_copy(0, 0).start()
-        got_z[0] = message[1]
-        wait_all(got_z.at[pl.ds(1, N_Z - 1)], z_recv)
+        send_z(1, 1)
 
     @pl.when(core == 0)
     def _():
-        for d in range(1, PLANE, 2):
+        for d in range(3, PLANE, 2):
             plane_copy(d).start()
-        wait_all(got_z, z_recv)
-
-    high, low = sum_messages([got_z[i] for i in range(N_Z)])
+        pl.semaphore_wait(ready.at[3], 1)
+        send_z(0, 0)
+
+    wait_all(got_z.at[pl.ds(1, 2 * N_Z - 1)], z_recv)
+    high, low = sum_messages([got_z[i] for i in range(2 * N_Z)])
     gram[0] = high
     gram[1] = low
 
@@ -532,14 +559,8 @@
                 for kind in range(2):
                     x_copy(step, kind, side).wait_send()
 
-    @pl.when(core == 1)
-    def _():
-        wait_all(got_plane.at[pl.ds(0, 15)], p_send)
-        wait_all(got_plane.at[pl.ds(0, 2 * N_Z - 1)], z_send)
-
-    @pl.when(core == 0)
-    def _():
-        wait_all(got_plane.at[pl.ds(0, 16)], p_send)
+    wait_all(got_plane.at[pl.ds(0, 15)], p_send)
+    wait_all(got_z.at[pl.ds(1, 2 * N_Z - 1)], z_send)
 
 
 def finish(basis_ref, gram_ref, q_hbm, r_hbm, up_hbm, q_ref, r_ref, up_ref, sem):
@@ -605,6 +626,8 @@
             pltpu.VMEM((ELEM_DEV, WIDTH), F32),
             pltpu.VMEM((ELEM_DEV, WIDTH, WIDTH), F32),
             pltpu.VMEM((ELEM_DEV, 6, FACE_WIDTH, FACE_WIDTH), F32),
+            pltpu.VMEM((ELEM_DEV, WIDTH, 128), F32),
+            pltpu.VMEM((ELEM_DEV, WIDTH, 128), F32),
             pltpu.VMEM((8, 384), F32),
             pltpu.VMEM((6,) + tile, F32),
             pltpu.VMEM((2, 2, 2) + tile, F32),
@@ -615,8 +638,8 @@
             pltpu.VMEM((2, 3, FACE_WIDTH, 128), F32),
             pltpu.VMEM((2, ELEM_DEV, FACE_WIDTH, 128), F32),
             pltpu.VMEM((2,) + tile, F32),
-            pltpu.VMEM((PLANE - 1,) + tile, F32),
-            pltpu.VMEM((N_Z,) + tile, F32),
+            pltpu.VMEM((PLANE - 2,) + tile, F32),
+            pltpu.VMEM((2 * N_Z,) + tile, F32),
             pltpu.SemaphoreType.DMA((4,)),
             pltpu.SemaphoreType.DMA((2,)),
             pltpu.SemaphoreType.DMA((2,)),
@@ -626,7 +649,7 @@
             pltpu.SemaphoreType.DMA,
             pltpu.SemaphoreType.DMA,
             pltpu.SemaphoreType.DMA,
-            pltpu.SemaphoreType.REGULAR((3,)),
+            pltpu.SemaphoreType.REGULAR((4,)),
         ],
         compiler_params=pltpu.CompilerParams(
             collective_id=0, has_side_effects=True, vmem_limit_bytes=24 * 2**20

time: 39.8 us -> 38.8 us (0.975)
  Pallas kernels: 39 us -> 38 us
    pallas_call x1, Pallas kernels: 38.1 us -> 37.1 us  [body(): pl.pallas_call(kernel, out_shape=(pltpu.VMEM((ELEM_DEV, 8, 384), F32), pl...]
where the time goes in v5:
time: 38.8 us; the launch traced here: 38.6 us
  Pallas kernels  38 us (98%)
  between operations  0.64 us (2%)
    pallas_call x1, Pallas kernels, body(): pl.pallas_call(kernel, out_shape=(pltpu.VMEM((ELEM_DEV, 8, 384), F32), pl...  37.1 us
    pallas_call x1, Pallas kernels, body(): pl.pallas_call(finish, out_shape=(jax.ShapeDtypeStruct((BASIS, ELEM_DEV,...  0.94 us

profile of v5, /device:TPU:1, one launch (start us, length us, event | category | flops | bytes accessed | tf_op | source)
XLA Modules:
  0.0 38.6 jit_solution(7172919671885708104)
XLA Ops:
  0.6 37.1 %shard_map.67 = (f32[4,8,384]{2,1,0:T(8,128)S(1)}, f32[2,8,128]{2,1,0:T(8,128)S(1)}) custom-call(s32[4,6]{1,0:T(4,128)} %nb_hbm.1, f32[4,320]{1,0:T(4,128)} %rhs_hbm.1, f32[4,320,320]{2,1,0:T(8,128)} %diag_hbm.1, f32[4,6,80,80]{3,2,1,0:T(8,128)} %face_hbm.1), custom_call_target="tpu_custom_call" | custom-call | tf_op jit(solution)/shard_map/pallas_call | solution.py:616
  37.7 0.9 %shard_map.68 = (f32[5,4,320]{2,1,0:T(4,128)}, f32[5,5]{1,0:T(8,128)}, f32[4,320]{1,0:T(4,128)}) custom-call(f32[4,8,384]{2,1,0:T(8,128)S(1)} %get-tuple-element.8.basis_ref, f32[2,8,128]{2,1,0:T(8,128)S(1)} %get-tuple-element.9.gram_ref), custom_call_target="tpu_custom_call" | custom-call | tf_op jit(solution)/shard_map/pallas_call | solution.py:658
